TPU v7x, 32 devices: a whole 2x2x4 slice. The times are simulated.
32 devices in a mesh: groups: 2 (over x), ctx: 16 (over z, y, core).
Axes of the slice: x: 2, y: 2, z: 4, core: 2. Of those that a mesh axis runs over, the one named last changes fastest.
Arguments:
- queries: bfloat16 [4096, 2048], P(('groups', 'ctx')), parts along dimension 0, may hold values from -90 to 90
- keys: bfloat16 [4096, 128], P(('groups', 'ctx')), parts along dimension 0, may hold values from -6 to 6
- values: bfloat16 [4096, 128], P(('groups', 'ctx')), parts along dimension 0, may hold values from -6 to 6
- cache_lengths: int32 [16], P('groups'), parts along dimension 0, may hold values from 1 to 1024, as said below
- query_lengths: int32 [16], P('groups'), parts along dimension 0, may hold values from 1 to 1024, as said below
Outputs:
- attended: bfloat16 [4096, 2048], P(('groups', 'ctx')), parts along dimension 0
- log_total: float32 [4096, 16], P(('groups', 'ctx')), parts along dimension 0
There are 2 independent parts, one for each index of `groups`. A program takes and returns all parts, laid end to end along the dimension named above; each array names one. Nothing has to cross between parts.
Inputs may be any that keep to these rules, and one draw needn't show every extreme that they name: `cache_lengths`: Positive, summing to 2048; the largest is exactly 1024. `query_lengths`: Positive, summing to 2048; the largest is exactly 1024.
All inputs are finite; a program needn't handle non-finite values.
Results may differ from a plain program's by a relative error of at most 0.0045.
Values may be sent and summed in bfloat16 or wider, within the bound.
A program may use at most 64 MiB of HBM per device.

v0:
```python
import math

import jax
import jax.numpy as jnp
from jax import lax
from jax.sharding import PartitionSpec as P

NEG_FILL = -1e30


def request_of(positions, lengths):
    ends = jnp.cumsum(lengths)[:-1]
    return jnp.sum((positions[:, None] >= ends[None, :]).astype(jnp.int32), axis=1)


def shards(queries, keys, values, cache_lengths, query_lengths):
    q_dev = queries.shape[0]
    width = keys.shape[1]
    heads = queries.shape[1] // width
    here = lax.axis_index("ctx")
    rows = queries.reshape(q_dev * heads, width)
    query_req = request_of(here * q_dev + jnp.arange(q_dev, dtype=jnp.int32), query_lengths)
    row_req = jnp.repeat(query_req, heads)
    scale = width ** (-0.5)

    def attend(carry, key_block, value_block, start):
        positions = start + jnp.arange(key_block.shape[0], dtype=jnp.int32)
        cache_req = request_of(positions, cache_lengths)
        top, total, mixed = carry
        score = jnp.dot(rows, key_block.T, preferred_element_type=jnp.float32) * scale
        mask = (row_req[:, None] == cache_req[None, :]) & True
        score = jnp.where(mask, score, NEG_FILL)
        new_top = jnp.maximum(top, jnp.max(score, axis=1))
        factor = jnp.exp(top - new_top)
        weight = jnp.where(mask, jnp.exp(score - new_top[:, None]), 0.0)
        total = total * factor + jnp.sum(weight, axis=1)
        mixed = mixed * factor[:, None] + jnp.dot(
            weight.astype(jnp.bfloat16), value_block, preferred_element_type=jnp.float32
        )
        return (new_top, total, mixed)

    start_state = (
        jnp.full((q_dev * heads,), NEG_FILL, jnp.float32),
        jnp.zeros((q_dev * heads,), jnp.float32),
        jnp.zeros((q_dev * heads, width), jnp.float32),
    )
    key_piece = lax.all_gather(keys, "ctx", axis=0, tiled=True)
    value_piece = lax.all_gather(values, "ctx", axis=0, tiled=True)
    length = key_piece.shape[0]
    block = math.gcd(length, 1024)
    nblocks = length // block

    def one_step(index, state):
        key_block = lax.dynamic_slice_in_dim(key_piece, index * block, block, 0)
        value_block = lax.dynamic_slice_in_dim(value_piece, index * block, block, 0)
        return attend(state, key_block, value_block, index * block)

    top, total, mixed = lax.fori_loop(0, nblocks, one_step, start_state)
    attended = (mixed / total[:, None]).astype(jnp.bfloat16).reshape(q_dev, heads * width)
    log_total = (top + jnp.log(total)).reshape(q_dev, heads)
    return (attended, log_total)


def solution(mesh):
    in_specs = (
        P(("groups", "ctx"), None),
        P(("groups", "ctx"), None),
        P(("groups", "ctx"), None),
        P("groups"),
        P("groups"),
    )
    out_specs = (P(("groups", "ctx"), None), P(("groups", "ctx"), None))
    return jax.shard_map(shards, mesh=mesh, in_specs=in_specs, out_specs=out_specs, check_vma=False)
```

profile of v0, /device:TPU:0, one launch (start us, length us, event | category | flops | bytes accessed | tf_op | source)
XLA Modules:
  0.0 64.0 jit_solution(3821850923970895720)
XLA Ops:
  0.6 0.8 %reduce-window.15 = s32[8,1]{0,1:T(1,128)S(1)} reduce-window(s32[8,1]{0,1:T(1,128)} %bitcast.30, s32[]{:T(128)} %constant.83.clone.1), window={size=8x1 pad=7_0x0_0}, to_apply=%region_2.3 | reduce-window | flops 56 | bytes 68 | tf_op jit(solution)/shard_map/reduce-window.4
  1.5 0.8 %reduce-window.14 = s32[8,1]{0,1:T(1,128)S(1)} reduce-window(s32[8,1]{0,1:T(1,128)} %bitcast.31, s32[]{:T(128)} %constant.83.clone.1), window={size=8x1 pad=7_0x0_0}, to_apply=%region_0.0 | reduce-window | flops 56 | bytes 68 | tf_op jit(solution)/shard_map/reduce-window
  2.3 0.1 convert_reduce_fusion.1
  2.4 1.3 %reshape.46 = bf16[2048,128]{1,0:T(8,128)(2,1)S(1)} reshape(bf16[128,2048]{1,0:T(8,128)(2,1)} %param.7) | data formatting | bytes 1048576 | tf_op jit(solution)/shard_map/reshape | solution.py:21
  3.7 24.8 %all_gather.6 = bf16[2048,128]{1,0:T(8,128)(2,1)S(1)} all-gather(bf16[128,128]{1,0:T(8,128)(2,1)} %param.8), channel_id=1, replica_groups=mesh['groups'=2,'ctx'=16] {'ctx'}, dimensions={0}, use_global_device_ids=true | all-gather | bytes 557056 | tf_op jit(solution)/shard_map/all_gather | solution.py:47
  28.5 19.1 %all_gather.7 = bf16[2048,128]{1,0:T(8,128)(2,1)S(1)} all-gather(bf16[128,128]{1,0:T(8,128)(2,1)} %param.9), channel_id=1, replica_groups=mesh['groups'=2,'ctx'=16] {'ctx'}, dimensions={0}, use_global_device_ids=true | all-gather | bytes 557056 | tf_op jit(solution)/shard_map/all_gather | solution.py:48
  47.6 14.2 %while.20 = (s32[]{:T(128)}, f32[2048]{0:T(1024)S(1)}, f32[2048]{0:T(1024)S(1)}, f32[2048,128]{1,0:T(8,128)S(1)}, s32[8,1]{0,1:T(1,128)S(1)}, /*index=5*/bf16[20...) while((s32[]{:T(128)}, f32[2048]{0:T(1024)S(1)}, ...), condition=%wide.region_7.8_spmd.clone, body=%wide.region_3.7_spmd.clone.sunk | while | flops 1108114432 | bytes 28517148 | solution.py:58
  47.6 0.1 convert_reduce_fusion.3
  47.7 0.1 broadcast_in_dim.81
  47.8 0.1 eq.93
  47.8 1.3 %fusion.30 = (f32[2048]{0:T(1024)S(1)}, f32[1024,2048]{1,0:T(8,128)S(1)}) fusion(s32[2048]{0:T(1024)S(1)} %eq.93, s32[1024]{0:T(1024)S(1)} %convert_reduce_fusion.3, bf16[2048,128]{1,0:T(8,128)(2,1)S(1)} %get-tuple-element.373, bf16[2048,128]{1,0:T(8,128)(2,1)S(1)} %get-tuple-element.372, s32[]{:T(128)S(6)} %select_n.63), kind=kOutput, calls=%fused_computation.3.clone.1 | convolution fusion | flops 545257472 | bytes 9195524 | tf_op jit(solution)/shard_map/while/body/eval_jaxpr/dot_general | solution.py:30
  49.2 2.7 %fusion.31 = f32[2048]{0:T(1024)S(1)} fusion(f32[1024,2048]{1,0:T(8,128)S(1)} %get-tuple-element.338, f32[2048]{0:T(1024)S(1)} %select_maximum_fusion.2, s32[2048]{0:T(1024)S(1)} %eq.93, s32[1024]{0:T(1024)S(1)} %convert_reduce_fusion.3), kind=kLoop, calls=%fused_computation.5.clone.1 | loop fusion | flops 12580864 | bytes 8417280 | tf_op jit(solution)/shard_map/while/body/eval_jaxpr/reduce_sum | solution.py:36
  51.9 2.8 %fusion.33 = f32[2048,128]{1,0:T(8,128)S(1)} fusion(f32[1024,2048]{1,0:T(8,128)S(1)} %get-tuple-element.338, f32[2048]{0:T(1024)S(1)} %select_maximum_fusion.2, s32[2048]{0:T(1024)S(1)} %eq.93, s32[1024]{0:T(1024)S(1)} %convert_reduce_fusion.3, f32[2048,128]{1,0:T(8,128)S(1)} %get-tuple-element.357, f32[2048]{0:T(1024)S(1)} %get-tuple-element.340, ...), kind=kOutput, calls=%fused_computation.7.clone.1 | convolution fusion | flops 550240256 | bytes 10776581 | tf_op jit(solution)/shard_map/while/body/eval_jaxpr/dot_general | solution.py:37
  54.7 0.1 convert_reduce_fusion.3
  54.8 0.1 broadcast_in_dim.81
  54.9 0.1 eq.93
  55.0 1.3 %fusion.30 = (f32[2048]{0:T(1024)S(1)}, f32[1024,2048]{1,0:T(8,128)S(1)}) fusion(s32[2048]{0:T(1024)S(1)} %eq.93, s32[1024]{0:T(1024)S(1)} %convert_reduce_fusion.3, bf16[2048,128]{1,0:T(8,128)(2,1)S(1)} %get-tuple-element.373, bf16[2048,128]{1,0:T(8,128)(2,1)S(1)} %get-tuple-element.372, s32[]{:T(128)S(6)} %select_n.63), kind=kOutput, calls=%fused_computation.3.clone.1 | convolution fusion | flops 545257472 | bytes 9195524 | tf_op jit(solution)/shard_map/while/body/eval_jaxpr/dot_general | solution.py:30
  56.3 2.7 %fusion.31 = f32[2048]{0:T(1024)S(1)} fusion(f32[1024,2048]{1,0:T(8,128)S(1)} %get-tuple-element.338, f32[2048]{0:T(1024)S(1)} %select_maximum_fusion.2, s32[2048]{0:T(1024)S(1)} %eq.93, s32[1024]{0:T(1024)S(1)} %convert_reduce_fusion.3), kind=kLoop, calls=%fused_computation.5.clone.1 | loop fusion | flops 12580864 | bytes 8417280 | tf_op jit(solution)/shard_map/while/body/eval_jaxpr/reduce_sum | solution.py:36
  59.0 2.8 %fusion.33 = f32[2048,128]{1,0:T(8,128)S(1)} fusion(f32[1024,2048]{1,0:T(8,128)S(1)} %get-tuple-element.338, f32[2048]{0:T(1024)S(1)} %select_maximum_fusion.2, s32[2048]{0:T(1024)S(1)} %eq.93, s32[1024]{0:T(1024)S(1)} %convert_reduce_fusion.3, f32[2048,128]{1,0:T(8,128)S(1)} %get-tuple-element.357, f32[2048]{0:T(1024)S(1)} %get-tuple-element.340, ...), kind=kOutput, calls=%fused_computation.7.clone.1 | convolution fusion | flops 550240256 | bytes 10776581 | tf_op jit(solution)/shard_map/while/body/eval_jaxpr/dot_general | solution.py:37
  61.8 0.3 divide_convert_fusion
  62.2 1.0 %reshape.47 = bf16[128,2048]{1,0:T(8,128)(2,1)} reshape(bf16[2048,128]{1,0:T(8,128)(2,1)S(1)} %divide_convert_fusion) | data formatting | bytes 1048576 | tf_op jit(solution)/shard_map/reshape | solution.py:59
  63.2 0.1 reshape.48
  63.3 0.7 %copy.8 = f32[128,16]{0,1:T(8,128)} copy(f32[128,16]{1,0:T(8,128)S(1)} %reshape.48) | data formatting | bytes 16384
  (16 shorter events, 0.1 us)
where the time goes:
time: 64.2 us; the launch traced here: 64 us
  blocking collectives  43.9 us (68%)
  matrix products  8.24 us (13%)
  other arithmetic  7.64 us (12%)
  local copies, waits for them, and re-layouts  3.38 us (5%)
  between operations  0.68 us (1%)
    all_gather x1, blocking collectives, shards(): key_piece = lax.all_gather(keys, 'ctx', axis=0, tiled=True)  24.8 us
    all_gather x1, blocking collectives, shards(): value_piece = lax.all_gather(values, 'ctx', axis=0, tiled=True)  19.1 us
    dot_general x2, matrix products, attend(): jnp.dot(weight.astype(jnp.bfloat16), value_block, preferred_element_type=...  5.61 us
    reduce_sum x2, other arithmetic, attend(): total = total * factor + jnp.sum(weight, axis=1)  5.33 us
    dot_general x2, matrix products, attend(): jnp.dot(rows, key_block.T, preferred_element_type=jnp.float32) * scale  2.62 us
    another operation x2, other arithmetic  1.66 us

commit v1 on v0

v1 whole, which is shorter than its diff:
```python
import functools
import math

import jax
import jax.numpy as jnp
from jax import lax
from jax.experimental import pallas as pl
from jax.experimental.pallas import tpu as pltpu
from jax.sharding import PartitionSpec as P

MESH = pl.DeviceIdType.MESH
APART = -(2.0**100)
LOWEST = -(2.0**90)
ROWS = 512


def flip(index, mask):
    out, bit = index, 1
    while bit <= mask:
        if mask & bit:
            out = out + bit - 2 * bit * lax.rem(lax.div(index, bit), 2)
        bit *= 2
    return out


def bounds(lengths_ref, lane):
    count = lengths_ref.shape[0]
    first = jnp.full(lane.shape, 2**30, jnp.int32)
    last = jnp.full(lane.shape, 2**30, jnp.int32)
    at = jnp.int32(0)
    for r in range(count):
        first = jnp.where(lane == r, at, first)
        at = at + lengths_ref[r]
        if r < count - 1:
            last = jnp.where(lane == r, at, last)
    return first, last


def kernel(n, q_hbm, k_hbm, v_hbm, clen, qlen, out_ref, log_ref,
           qbuf, kbuf, vbuf, acc, top, local_sem, send_sem, recv_sem):
    me = lax.axis_index("ctx")
    tokens, block = out_ref.shape[0], k_hbm.shape[0]
    width = k_hbm.shape[1]
    heads = out_ref.shape[1] // width
    count = clen.shape[0]
    zs = n // 4
    peers = [1, 2] + [4 * k for k in range(1, zs)]

    barrier = pltpu.get_barrier_semaphore()
    for j in peers:
        pl.semaphore_signal(barrier, inc=1, device_id={"ctx": flip(me, j)}, device_id_type=MESH)
    own_k = pltpu.make_async_copy(k_hbm, kbuf.at[0:block, 0:width], local_sem.at[0])
    own_v = pltpu.make_async_copy(v_hbm, vbuf.at[0:block, 0:width], local_sem.at[1])
    own_k.start()
    own_v.start()
    own_q = []
    for h in range(heads):
        copy = pltpu.make_async_copy(
            q_hbm.at[:, h * width:(h + 1) * width],
            qbuf.at[h * tokens:(h + 1) * tokens, 0:width],
            local_sem.at[2 + h])
        copy.start()
        own_q.append(copy)
    own_k.wait()
    own_v.wait()
    pl.semaphore_wait(barrier, len(peers))

    sends = []

    def send(slot, hop):
        to = slot ^ hop
        for i, buf in enumerate((kbuf, vbuf)):
            copy = pltpu.make_async_remote_copy(
                src_ref=buf.at[slot * block:(slot + 1) * block, 0:width],
                dst_ref=buf.at[to * block:(to + 1) * block, 0:width],
                send_sem=send_sem.at[i, to],
                recv_sem=recv_sem.at[i, to],
                device_id={"ctx": flip(me, hop)},
                device_id_type=MESH)
            copy.start()
            sends.append(copy)

    def arrived(slot):
        for i, buf in enumerate((kbuf, vbuf)):
            there = buf.at[slot * block:(slot + 1) * block, 0:width]
            pltpu.make_async_remote_copy(
                src_ref=there, dst_ref=there,
                send_sem=send_sem.at[i, slot], recv_sem=recv_sem.at[i, slot],
                device_id={"ctx": flip(me, 1)}, device_id_type=MESH).wait_recv()

    for j in peers:
        send(0, j)

    lane = lax.broadcasted_iota(jnp.int32, (1, width), 1)
    q_first, q_last = bounds(qlen, lane)
    k_first, k_last = bounds(clen, lane)
    row = lax.broadcasted_iota(jnp.int32, (tokens, width), 0) + me * tokens
    inside = (row >= q_first) & (row < q_last)
    apart = jnp.where(inside | (lane >= count), 0.0, APART).astype(jnp.bfloat16)
    for h in range(heads):
        qbuf[h * tokens:(h + 1) * tokens, width:] = apart
    vbuf[:, width:] = jnp.ones((n * block, width), jnp.bfloat16)
    spot = lax.broadcasted_iota(jnp.int32, (block, width), 0)
    for j in range(n):
        key = spot + flip(me, j) * block
        kbuf[j * block:(j + 1) * block, width:] = jnp.where(
            (key >= k_first) & (key < k_last), 1.0, 0.0).astype(jnp.bfloat16)
    for copy in own_q:
        copy.wait()

    factor2 = math.log2(math.e) * width ** -0.5
    span = 4 * block

    def attend(phase):
        keys = kbuf[phase * span:(phase + 1) * span, :]
        values = vbuf[phase * span:(phase + 1) * span, :]

        def rows(i, _):
            at = pl.ds(pl.multiple_of(i * ROWS, ROWS), ROWS)
            score = lax.dot_general(qbuf[at, :], keys, (((1,), (1,)), ((), ())),
                                    preferred_element_type=jnp.float32)
            most = jnp.max(score, axis=1, keepdims=True)
            if phase == 0:
                new = jnp.maximum(most, LOWEST)
            else:
                old = top[at, :]
                new = jnp.maximum(old[:, 0:1], most)
            weight = jnp.exp2((score - new) * factor2).astype(jnp.bfloat16)
            mixed = jnp.dot(weight, values, preferred_element_type=jnp.float32)
            if phase > 0:
                less = jnp.exp2((old - new) * factor2)
                mixed = jnp.concatenate([acc[at, 0:width] * less, acc[at, width:] * less], axis=1) + mixed
            acc[at, :] = mixed
            top[at, :] = jnp.broadcast_to(new, (ROWS, width))
            return 0

        lax.fori_loop(0, heads * tokens // ROWS, rows, 0)

    def forward(k):
        arrived(4 * k)
        send(4 * k, 2)
        send(4 * k, 1)

    def share(k):
        arrived(4 * k + 2)
        send(4 * k + 2, 1)

    share(0)
    if zs > 1:
        forward(1)
    for k in range(zs):
        arrived(4 * k + 1)
        arrived(4 * k + 3)
        if k + 1 < zs:
            share(k + 1)
        if k + 2 < zs:
            forward(k + 2)
        attend(k)

    logs = jnp.zeros((tokens, heads), jnp.float32)
    head_lane = lax.broadcasted_iota(jnp.int32, (tokens, heads), 1)
    for h in range(heads):
        at = slice(h * tokens, (h + 1) * tokens)
        total = acc[at, width:]
        out_ref[:, h * width:(h + 1) * width] = (acc[at, 0:width] / total).astype(jnp.bfloat16)
        log = top[at, 0:1] * (width ** -0.5) + jnp.log(total[:, 0:1])
        logs = jnp.where(head_lane == h, log, logs)
    log_ref[...] = logs
    for copy in sends:
        copy.wait_send()


def shards(n, queries, keys, values, cache_lengths, query_lengths):
    tokens, flat = queries.shape
    block, width = keys.shape
    heads = flat // width
    return pl.pallas_call(
        functools.partial(kernel, n),
        out_shape=(jax.ShapeDtypeStruct((tokens, flat), jnp.bfloat16),
                   jax.ShapeDtypeStruct((tokens, heads), jnp.float32)),
        in_specs=[pl.BlockSpec(memory_space=pl.ANY)] * 3 + [pl.BlockSpec(memory_space=pltpu.SMEM)] * 2,
        out_specs=(pl.BlockSpec(memory_space=pltpu.VMEM),) * 2,
        scratch_shapes=[
            pltpu.VMEM((heads * tokens, 2 * width), jnp.bfloat16),
            pltpu.VMEM((n * block, 2 * width), jnp.bfloat16),
            pltpu.VMEM((n * block, 2 * width), jnp.bfloat16),
            pltpu.VMEM((heads * tokens, 2 * width), jnp.float32),
            pltpu.VMEM((heads * tokens, width), jnp.float32),
            pltpu.SemaphoreType.DMA((2 + heads,)),
            pltpu.SemaphoreType.DMA((2, n)),
            pltpu.SemaphoreType.DMA((2, n)),
        ],
        compiler_params=pltpu.CompilerParams(
            collective_id=0, has_side_effects=True, vmem_limit_bytes=48 * 2**20),
        cost_estimate=pl.CostEstimate(
            flops=4 * heads * tokens * n * block * width,
            bytes_accessed=4 * tokens * flat + 4 * block * width,
            transcendentals=heads * tokens * n * block),
    )(queries, keys, values, cache_lengths, query_lengths)


def solution(mesh):
    in_specs = (
        P(("groups", "ctx"), None),
        P(("groups", "ctx"), None),
        P(("groups", "ctx"), None),
        P("groups"),
        P("groups"),
    )
    out_specs = (P(("groups", "ctx"), None), P(("groups", "ctx"), None))
    body = functools.partial(shards, mesh.shape["ctx"])
    return jax.shard_map(body, mesh=mesh, in_specs=in_specs, out_specs=out_specs, check_vma=False)
```

time: 64.2 us -> 38.9 us (0.61)
  blocking collectives: 43.9 us -> 0 us
  Pallas kernels: 0 us -> 32.6 us
  matrix products: 8.24 us -> 0 us
  other arithmetic: 7.64 us -> 0 us
  local copies, waits for them, and re-layouts: 3.38 us -> 5.32 us
    all_gather x2 -> x0, blocking collectives: 43.9 us -> none  [the longest x1 24.8 us: shards(): key_piece = lax.all_gather(keys, 'ctx', axis=0, tiled=True)]
    pallas_call x0 -> x1, Pallas kernels: none -> 32.6 us  [shards(): pl.pallas_call(functools.partial(kernel, n), out_shape=(jax.ShapeDtypeStr...]
    dot_general x4 -> x0, matrix products: 8.24 us -> none  [the longest x2 5.61 us: attend(): jnp.dot(weight.astype(jnp.bfloat16), value_block, preferred_element_type=...]
    reduce_sum x5 -> x0, other arithmetic: 5.58 us -> none  [the longest x2 5.33 us: attend(): total = total * factor + jnp.sum(weight, axis=1)]
    unnamed x1 -> x11, local copies, waits for them, and re-layouts: 0.67 us -> 4.65 us
    reshape x3 -> x0, local copies, waits for them, and re-layouts: 2.37 us -> none  [the longest x1 1.28 us: shards(): rows = queries.reshape(q_dev * heads, width)]
    another operation x2 -> x0, other arithmetic: 1.66 us -> none
    pallas_call x0 -> x1, local copies, waits for them, and re-layouts: none -> 0.67 us  [shards(): pl.pallas_call(functools.partial(kernel, n), out_shape=(jax.ShapeDtypeStr...]
where the time goes in v1:
time: 38.9 us; the launch traced here: 38.5 us
  Pallas kernels  32.6 us (84%)
  local copies, waits for them, and re-layouts  5.32 us (14%)
  between operations  0.65 us (2%)
    pallas_call x1, Pallas kernels, shards(): pl.pallas_call(functools.partial(kernel, n), out_shape=(jax.ShapeDtypeStr...  32.6 us
    unnamed x11, local copies, waits for them, and re-layouts  4.65 us

profile of v1, /device:TPU:0, one launch (start us, length us, event | category | flops | bytes accessed | tf_op | source)
XLA Modules:
  0.0 38.5 jit_solution(8711873302254106433)
XLA Ops:
  0.6 0.0 copy-start
  0.6 1.0 %copy-done = bf16[128,2048]{1,0:T(8,128)(2,1)S(1)} copy-done((bf16[128,2048]{1,0:T(8,128)(2,1)S(1)}, bf16[128,2048]{1,0:T(8,128)(2,1)}, u32[]{:S(2)}) %copy-start) | copy-done | bytes 524312
  1.7 0.0 copy-start.1
  1.7 0.8 %copy-done.1 = bf16[128,128]{1,0:T(8,128)(2,1)S(1)} copy-done((bf16[128,128]{1,0:T(8,128)(2,1)S(1)}, bf16[128,128]{1,0:T(8,128)(2,1)}, u32[]{:S(2)}) %copy-start.1) | copy-done | bytes 32792
  2.4 0.0 copy-start.2
  2.4 0.8 %copy-done.2 = bf16[128,128]{1,0:T(8,128)(2,1)S(1)} copy-done((bf16[128,128]{1,0:T(8,128)(2,1)S(1)}, bf16[128,128]{1,0:T(8,128)(2,1)}, u32[]{:S(2)}) %copy-start.2) | copy-done | bytes 32792
  3.2 0.0 copy-start.3
  3.2 0.7 %copy-done.3 = s32[8]{0:T(128)S(1)} copy-done((s32[8]{0:T(128)S(1)}, s32[8]{0:T(128)}, u32[]{:S(2)}) %copy-start.3) | copy-done | bytes 56
  3.8 0.0 copy-start.4
  3.8 0.7 %copy-done.4 = s32[8]{0:T(128)S(1)} copy-done((s32[8]{0:T(128)S(1)}, s32[8]{0:T(128)}, u32[]{:S(2)}) %copy-start.4) | copy-done | bytes 56
  4.5 32.6 %shard_map.68 = (bf16[128,2048]{1,0:T(8,128)(2,1)S(1)}, f32[128,16]{1,0:T(8,128)S(1)}) custom-call(bf16[128,2048]{1,0:T(8,128)(2,1)S(1)} %copy-done, bf16[128,128]{1,0:T(8,128)(2,1)S(1)} %copy-done.1, bf16[128,128]{1,0:T(8,128)(2,1)S(1)} %copy-done.2, s32[8]{0:T(128)S(1)} %copy-done.3, s32[8]{0:T(128)S(1)} %copy-done.4), custom_call_target="tpu_custom_call" | custom-call | flops 2147483648 | bytes 1114112 | tf_op jit(solution)/shard_map/pallas_call | solution.py:177
  37.1 0.7 %copy.7 = f32[128,16]{0,1:T(8,128)} copy(f32[128,16]{1,0:T(8,128)S(1)} %get-tuple-element.3) | data formatting | bytes 16384 | tf_op jit(solution)/shard_map/pallas_call | solution.py:177
  37.7 0.8 %copy.9 = bf16[128,2048]{1,0:T(8,128)(2,1)} copy(bf16[128,2048]{1,0:T(8,128)(2,1)S(1)} %get-tuple-element.6) | data formatting | bytes 1048576
Async XLA Ops:
  0.6 1.0 %copy-start = (bf16[128,2048]{1,0:T(8,128)(2,1)S(1)}, bf16[128,2048]{1,0:T(8,128)(2,1)}, u32[]{:S(2)}) copy-start(bf16[128,2048]{1,0:T(8,128)(2,1)} %q_hbm.1) | copy-start | bytes 1572868
  1.7 0.8 %copy-start.1 = (bf16[128,128]{1,0:T(8,128)(2,1)S(1)}, bf16[128,128]{1,0:T(8,128)(2,1)}, u32[]{:S(2)}) copy-start(bf16[128,128]{1,0:T(8,128)(2,1)} %k_hbm.1) | copy-start | bytes 98308
  2.4 0.8 %copy-start.2 = (bf16[128,128]{1,0:T(8,128)(2,1)S(1)}, bf16[128,128]{1,0:T(8,128)(2,1)}, u32[]{:S(2)}) copy-start(bf16[128,128]{1,0:T(8,128)(2,1)} %v_hbm.1) | copy-start | bytes 98308
  3.2 0.7 %copy-start.3 = (s32[8]{0:T(128)S(1)}, s32[8]{0:T(128)}, u32[]{:S(2)}) copy-start(s32[8]{0:T(128)} %clen.1) | copy-start | bytes 100
  3.8 0.7 %copy-start.4 = (s32[8]{0:T(128)S(1)}, s32[8]{0:T(128)}, u32[]{:S(2)}) copy-start(s32[8]{0:T(128)} %qlen.1) | copy-start | bytes 100
